TPU v7x, 32 devices: a whole 2x2x4 slice. The times are simulated.
32 devices in a mesh: group: 4 (over z), dev: 8 (over y, x, core).
Axes of the slice: x: 2, y: 2, z: 4, core: 2. Of those that a mesh axis runs over, the one named last changes fastest.
Arguments:
- start: float32 [512, 256], P(('group', 'dev')), may hold values from -12 to 12
- coords: float32 [512, 3, 256], P(('group', 'dev')), may hold values from -1 to 1
- area: float32 [512, 256], P(('group', 'dev')), may hold values from 0.1 to 0.4
- near_list: int32 [512, 6], P(('group', 'dev')), may hold values from -1 to 511, as said below
- basis: float32 [512, 64, 256], P(('group', 'dev')), may hold values from -0.375 to 0.375
- far_leaf: int32 [512, 8], P(('group', 'dev')), may hold values from 0 to 127
- couple_leaf: float32 [512, 64, 512], P(('group', 'dev')), may hold values from -0.25 to 0.25
- transfer: float32 [32, 64, 1024], P(('group', 'dev')), may hold values from -0.375 to 0.375
- far_top: int32 [32, 16], P(('group', 'dev')), may hold values from 0 to 31
- couple_top: float32 [32, 64, 1024], P(('group', 'dev')), may hold values from -0.1875 to 0.1875
Outputs:
- product_first: float32 [512, 256], P(('group', 'dev'))
- product_second: float32 [512, 256], P(('group', 'dev'))
Inputs may be any that keep to these rules, and one draw needn't show every extreme that they name: `near_list`: row i names leaf i once and otherwise leaves of the same group, none twice; -1 marks an unused entry. Over the rows of one device, the named leaves that lie on other devices come from exactly 4 devices, exactly 8 distinct leaves from each.
All inputs are finite; a program needn't handle non-finite values.
Results may differ from a plain program's by a relative error of at most 0.0003.
Values sent between devices are 32-bit elements; how exact they have to be, the bound alone decides.
A program may use at most 64 MiB of HBM per device.

v0:
```python
import math

import jax
import jax.numpy as jnp
from jax import lax
from jax.sharding import PartitionSpec as P

FOUR_PI = 4.0 * math.pi
SOFTENING = 0.01
EPSILON = 1e-06
HIGHEST_PRECISION = lax.Precision.HIGHEST


def near_block(targets, sources, weights):
    squared = (targets[:, None, 0, :, None] - sources[:, :, 0, None, :]) ** 2
    for component in (1, 2):
        squared = (
            squared
            + (targets[:, None, component, :, None] - sources[:, :, component, None, :]) ** 2
        )
    coupling = 1.0 / (FOUR_PI * jnp.sqrt(squared + SOFTENING))
    return jnp.einsum("bkij,bkj->bi", coupling, weights, precision=HIGHEST_PRECISION)


def per_device(
    start, coords, area, near_list, basis, far_leaf, couple_leaf, transfer, far_top, couple_top
):
    leaves = start.shape[0]
    panels = start.shape[1]
    entries = near_list.shape[1]
    coeffs = basis.shape[1]
    dev_count = lax.axis_size("dev")
    group_count = lax.axis_size("group")
    my_dev = lax.axis_index("dev")
    my_group = lax.axis_index("group")
    live = near_list >= 0
    relative = jnp.where(live, near_list - my_group * (dev_count * leaves), my_dev * leaves)
    alive = live.astype(jnp.float32)
    every_point = lax.all_gather(coords, "dev", axis=0, tiled=True)
    points = every_point[relative]

    def fetch(charges, flat_moments):
        group_charges, in_group = (
            lax.all_gather(charges, "dev", axis=0, tiled=True),
            lax.all_gather(flat_moments, "dev", axis=0, tiled=True),
        )
        return (group_charges[relative], in_group)

    blocks = leaves // 8

    def near_field(sources_charges):
        partner_charges = sources_charges * alive[:, :, None]

        def block_sum(pieces):
            targets, sources, weights = pieces
            return near_block(targets, sources, weights)

        result = lax.map(
            block_sum,
            (
                coords.reshape(blocks, 8, 3, panels),
                points.reshape(blocks, 8, entries, 3, panels),
                partner_charges.reshape(blocks, 8, entries, panels),
            ),
        )
        return result.reshape(leaves, panels)

    def far_finish(in_group, every_cluster):
        moment_table = in_group.reshape(dev_count * leaves, coeffs)
        partners = moment_table[far_leaf].reshape(leaves, -1)
        local = jnp.einsum("lrq,lq->lr", couple_leaf, partners, precision=HIGHEST_PRECISION)
        remote_clusters = every_cluster[far_top[0]].reshape(1, -1)
        level = jnp.einsum("drq,dq->dr", couple_top, remote_clusters, precision=HIGHEST_PRECISION)
        down = jnp.einsum("drq,dr->dq", transfer, level, precision=HIGHEST_PRECISION).reshape(
            leaves, coeffs
        )
        return jnp.einsum("lrj,lr->lj", basis, local + down, precision=HIGHEST_PRECISION)

    def apply_operator(vector):
        charges = area * vector
        moments = jnp.einsum("lrj,lj->lr", basis, charges, precision=HIGHEST_PRECISION)
        flat_moments = moments.reshape(1, leaves * coeffs)
        cluster = jnp.einsum("drq,dq->dr", transfer, flat_moments, precision=HIGHEST_PRECISION)
        every_cluster = lax.all_gather(cluster, ("group", "dev"), axis=0, tiled=True)
        near_charges, in_group = fetch(charges, flat_moments)
        near_part = near_field(near_charges)
        return near_part + far_finish(in_group, every_cluster)

    total_panels = leaves * panels * dev_count * group_count
    squares_start = lax.psum(jnp.sum(start * start), ("group", "dev"))
    unit_first = start / jnp.sqrt(squares_start / total_panels + EPSILON)
    product_first = apply_operator(unit_first)
    along, length_sq = lax.psum(
        (jnp.sum(unit_first * product_first), jnp.sum(unit_first * unit_first)), ("group", "dev")
    )
    projection = along / length_sq
    orthogonal = product_first - projection * unit_first
    squares_second = lax.psum(jnp.sum(orthogonal * orthogonal), ("group", "dev"))
    unit_second = orthogonal / jnp.sqrt(squares_second / total_panels + EPSILON)
    product_second = apply_operator(unit_second)
    return (product_first, product_second)


def solution(mesh):
    in_specs = (
        P(("group", "dev"), None),
        P(("group", "dev"), None, None),
        P(("group", "dev"), None),
        P(("group", "dev"), None),
        P(("group", "dev"), None, None),
        P(("group", "dev"), None),
        P(("group", "dev"), None, None),
        P(("group", "dev"), None, None),
        P(("group", "dev"), None),
        P(("group", "dev"), None, None),
    )
    out_specs = (P(("group", "dev"), None), P(("group", "dev"), None))
    return jax.shard_map(
        per_device, mesh=mesh, in_specs=in_specs, out_specs=out_specs, check_vma=False
    )
```

profile of v0, /device:TPU:0, one launch (start us, length us, event | category | flops | bytes accessed | tf_op | source)
XLA Modules:
  0.0 376.6 jit_solution(13749457830670418903)
XLA Ops:
  0.7 0.8 compare_select_fusion.1
  1.7 1.3 multiply_reduce_fusion.3
  3.0 42.2 %psum.28 = f32[]{:T(128)} all-reduce(f32[]{:T(128)} %multiply_reduce_fusion.3), channel_id=1, replica_groups=mesh['group'=4,'dev'=8] {'group','dev'}, use_global_device_ids=true, to_apply=%region_1.2 | all-reduce | flops 1 | bytes 8 | tf_op jit(solution)/shard_map/psum | solution.py:90
  45.9 0.7 fusion.42
  46.6 10.2 %all_gather.22 = f32[128,256]{1,0:T(8,128)S(1)} all-gather(f32[16,256]{1,0:T(8,128)S(1)} %fusion.42), channel_id=1, replica_groups=mesh['group'=4,'dev'=8] {'dev'}, dimensions={0}, use_global_device_ids=true | all-gather | bytes 147456 | tf_op jit(solution)/shard_map/all_gather | solution.py:44
  56.8 0.7 gather_fusion.1
  57.5 0.7 fusion.40
  58.3 0.7 broadcast_multiply_fusion.1
  59.0 8.8 %all_gather.21 = f32[128,3,256]{2,0,1:T(8,128)S(1)} all-gather(f32[16,3,256]{2,0,1:T(8,128)} %param.15), channel_id=1, replica_groups=mesh['group'=4,'dev'=8] {'dev'}, dimensions={0}, use_global_device_ids=true | all-gather | bytes 442368 | tf_op jit(solution)/shard_map/all_gather | solution.py:39
  68.2 0.8 gather_fusion
  69.1 41.7 %while.20 = (s32[]{:T(128)}, f32[2,8,256]{2,1,0:T(8,128)S(1)}, f32[2,8,3,256]{3,2,1,0:T(4,128)S(1)}, f32[2,8,6,3,256]{4,1,3,2,0:T(8,128)S(1)}, f32[2,8,6,256]{3,2,1,0:T(8,128)}, /*index=5*/s32[]{:T(128)}) while((s32[]{:T(128)}, f32[2,8,256]{2,1,0:T(8,128)S(1)}, f32[2,8,3,256]{3,2,1,0:T(4,128)S(1)}, f32[2,8,6,3,256]{4,1,3,2,0:T(8,128)S(1)}, ...), condition=%wide.region_3.4_spmd, body=%wide.region_2.3_spmd.sunk | while | flops 72351744 | bytes 1376341 | solution.py:58
  69.4 0.9 dynamic-slice_bitcast_fusion.14
  70.3 19.7 %fusion.73 = f32[8,1,256,1]{2,1,3,0:T(1,128)S(1)} fusion(f32[8,6,256]{2,1,0:T(8,128)S(1)} %copy.111, f32[8,256]{1,0:T(8,128)S(1)} %get-tuple-element.195, f32[8,6,256]{2,1,0:T(8,128)S(1)} %copy.112, f32[8,256]{1,0:T(8,128)S(1)} %get-tuple-element.197, f32[8,6,256]{2,1,0:T(8,128)S(1)} %copy.113, f32[8,256]{1,0:T(8,128)S(1)} %bitcast.158, ...), kind=kOutput, calls=%fused_computation.8.clone.1 | convolution fusion | flops 72351744 | bytes 229376 | tf_op jit(solution)/shard_map/while/body/eval_jaxpr/bkij,bkj->bi/dot_general | solution.py:22
  90.2 0.9 dynamic-slice_bitcast_fusion.14
  91.1 19.7 %fusion.73 = f32[8,1,256,1]{2,1,3,0:T(1,128)S(1)} fusion(f32[8,6,256]{2,1,0:T(8,128)S(1)} %copy.111, f32[8,256]{1,0:T(8,128)S(1)} %get-tuple-element.195, f32[8,6,256]{2,1,0:T(8,128)S(1)} %copy.112, f32[8,256]{1,0:T(8,128)S(1)} %get-tuple-element.197, f32[8,6,256]{2,1,0:T(8,128)S(1)} %copy.113, f32[8,256]{1,0:T(8,128)S(1)} %bitcast.158, ...), kind=kOutput, calls=%fused_computation.8.clone.1 | convolution fusion | flops 72351744 | bytes 229376 | tf_op jit(solution)/shard_map/while/body/eval_jaxpr/bkij,bkj->bi/dot_general | solution.py:22
  111.5 1.0 fusion.38
  112.5 1.2 convolution_bitcast_fusion.3
  114.0 39.3 %all-reduce = f32[2048]{0:T(1024)S(1)} all-reduce(f32[2048]{0:T(1024)S(1)} %dynamic-update-slice), channel_id=2, replica_groups=mesh['group'=4,'dev'=8] {'group','dev'}, use_global_device_ids=true, to_apply=%add | all-reduce | flops 2048 | bytes 16384
  154.6 1.2 convolution_bitcast_fusion.2
  155.8 1.9 dot_general.56
  157.7 1.5 fusion.30
  159.4 10.8 %all-gather.2 = f32[8,1,1024]{2,1,0:T(1,128)} all-gather(f32[1,1,1024]{2,1,0:T(1,128)S(1)} %reshape.217), channel_id=1, replica_groups=mesh['group'=4,'dev'=8] {'dev'}, dimensions={0}, use_global_device_ids=true | all-gather | bytes 36864 | tf_op jit(solution)/shard_map/all_gather | solution.py:45
  170.2 1.4 reduce
  171.6 0.8 reshape.127
  172.4 0.7 compare_select_fusion
  174.5 1.2 gather_fusion.2
  175.7 0.9 reshape.254
  176.7 1.8 fusion.45
  179.8 38.7 %all-reduce.2 = (f32[]{:T(128)}, f32[]{:T(128)}) all-reduce(f32[]{:T(128)} %get-tuple-element.79, f32[]{:T(128)} %get-tuple-element.78), channel_id=1, replica_groups=mesh['group'=4,'dev'=8] {'group','dev'}, use_global_device_ids=true, to_apply=%region_5.6 | all-reduce | flops 2 | bytes 16 | tf_op jit(solution)/shard_map/psum | solution.py:93
  220.4 41.1 %psum.31 = f32[]{:T(128)} all-reduce(f32[]{:T(128)} %multiply_reduce_fusion), channel_id=1, replica_groups=mesh['group'=4,'dev'=8] {'group','dev'}, use_global_device_ids=true, to_apply=%region_9.10 | all-reduce | flops 1 | bytes 8 | tf_op jit(solution)/shard_map/psum | solution.py:98
  262.2 0.7 divide_multiply_fusion
  263.0 1.0 fusion.36
  264.0 1.2 convolution_bitcast_fusion.1
  265.5 39.5 %all-reduce.1 = f32[2048]{0:T(1024)S(1)} all-reduce(f32[2048]{0:T(1024)S(1)} %dynamic-update-slice.1), channel_id=3, replica_groups=mesh['group'=4,'dev'=8] {'group','dev'}, use_global_device_ids=true, to_apply=%add.1 | all-reduce | flops 2048 | bytes 16384
  305.1 0.7 gather_fusion.6
  305.9 1.2 convolution_bitcast_fusion
  307.1 1.6 fusion.28
  308.8 9.8 %all-gather.3 = f32[8,1,1024]{2,1,0:T(1,128)S(1)} all-gather(f32[1,1,1024]{2,1,0:T(1,128)S(1)} %reshape.219), channel_id=1, replica_groups=mesh['group'=4,'dev'=8] {'dev'}, dimensions={0}, use_global_device_ids=true | all-gather | bytes 36864 | tf_op jit(solution)/shard_map/all_gather | solution.py:45
  318.6 0.7 reduce.1
  319.3 0.8 reshape.135
  320.1 1.2 gather_fusion.5
  321.3 1.5 reshape.258
  322.9 2.6 fusion.47
  326.1 9.0 %all_gather.25 = f32[128,256]{1,0:T(8,128)S(1)} all-gather(f32[16,256]{1,0:T(8,128)S(1)} %divide_multiply_fusion), channel_id=1, replica_groups=mesh['group'=4,'dev'=8] {'dev'}, dimensions={0}, use_global_device_ids=true | all-gather | bytes 147456 | tf_op jit(solution)/shard_map/all_gather | solution.py:44
  335.1 0.7 gather_fusion.4
  336.0 40.0 %while.21 = (s32[]{:T(128)}, f32[2,8,256]{2,1,0:T(8,128)S(1)}, f32[2,8,3,256]{3,2,1,0:T(4,128)S(1)}, f32[2,8,6,3,256]{4,1,3,2,0:T(8,128)S(1)}, f32[2,8,6,256]{3,2,1,0:T(8,128)S(1)}, /*index=5*/s32[]{:T(128)}) while((s32[]{:T(128)}, f32[2,8,256]{2,1,0:T(8,128)S(1)}, f32[2,8,3,256]{3,2,1,0:T(4,128)S(1)}, f32[2,8,6,3,256]{4,1,3,2,0:T(8,128)S(1)}, ...), condition=%wide.region_11.12_spmd, body=%wide.region_10.11_spmd.sunk | while | flops 72351744 | bytes 1376341 | solution.py:58
  336.2 19.8 %fusion.76 = f32[8,1,256,1]{2,1,3,0:T(1,128)S(1)} fusion(f32[8,6,256]{2,1,0:T(8,128)S(1)} %copy.118, f32[8,256]{1,0:T(8,128)S(1)} %get-tuple-element.208, f32[8,6,256]{2,1,0:T(8,128)S(1)} %copy.119, f32[8,256]{1,0:T(8,128)S(1)} %get-tuple-element.210, f32[8,6,256]{2,1,0:T(8,128)S(1)} %copy.120, f32[8,256]{1,0:T(8,128)S(1)} %bitcast.159, ...), kind=kOutput, calls=%fused_computation.33.clone.1 | convolution fusion | flops 72351744 | bytes 229376 | tf_op jit(solution)/shard_map/while/body/eval_jaxpr/bkij,bkj->bi/dot_general | solution.py:22
  356.2 19.8 %fusion.76 = f32[8,1,256,1]{2,1,3,0:T(1,128)S(1)} fusion(f32[8,6,256]{2,1,0:T(8,128)S(1)} %copy.118, f32[8,256]{1,0:T(8,128)S(1)} %get-tuple-element.208, f32[8,6,256]{2,1,0:T(8,128)S(1)} %copy.119, f32[8,256]{1,0:T(8,128)S(1)} %get-tuple-element.210, f32[8,6,256]{2,1,0:T(8,128)S(1)} %copy.120, f32[8,256]{1,0:T(8,128)S(1)} %bitcast.159, ...), kind=kOutput, calls=%fused_computation.33.clone.1 | convolution fusion | flops 72351744 | bytes 229376 | tf_op jit(solution)/shard_map/while/body/eval_jaxpr/bkij,bkj->bi/dot_general | solution.py:22
  (101 shorter events, 8.8 us)
Async XLA Ops:
  0.6 176.0 %copy-start = (f32[16,64,512]{2,1,0:T(8,128)S(1)}, f32[16,64,512]{2,1,0:T(8,128)}, u32[]{:S(2)}) copy-start(f32[16,64,512]{2,1,0:T(8,128)} %param.20) | copy-start | bytes 6291460
  56.8 12.3 %copy-start.5 = (f32[16,3,256]{2,0,1:T(8,128)S(1)}, f32[16,3,256]{2,0,1:T(8,128)}, u32[]{:S(2)}) copy-start(f32[16,3,256]{2,0,1:T(8,128)} %param.15) | copy-start | bytes 147460
  69.1 42.3 %copy-start.1 = (f32[16,64,256]{2,1,0:T(8,128)S(1)}, f32[16,64,256]{2,1,0:T(8,128)}, u32[]{:S(2)}) copy-start(f32[16,64,256]{2,1,0:T(8,128)} %param.18) | copy-start | bytes 3145732
  69.1 84.2 %copy-start.10 = (s32[1,16]{1,0:T(1,128)S(1)}, s32[1,16]{1,0:T(1,128)}, u32[]{:S(2)}) copy-start(s32[1,16]{1,0:T(1,128)} %param.22) | copy-start | bytes 196
  110.8 0.6 copy-start.7
  110.9 59.3 %copy-start.2 = (f32[2,8,3,256]{3,2,1,0:T(4,128)}, f32[2,8,3,256]{3,2,1,0:T(4,128)S(1)}, u32[]{:S(2)}) copy-start(f32[2,8,3,256]{3,2,1,0:T(4,128)S(1)} %get-tuple-element.250) | copy-start | bytes 147460
  153.4 0.6 copy-start.9
  159.3 19.9 %copy-start.4 = (f32[16,256]{1,0:T(8,128)S(1)}, f32[16,256]{1,0:T(8,128)}, u32[]{:S(2)}) copy-start(f32[16,256]{1,0:T(8,128)} %param.14) | copy-start | bytes 49156
  175.7 3.4 copy-start.8
  179.8 85.8 %copy-start.6 = (f32[16,256]{1,0:T(8,128)}, f32[16,256]{1,0:T(8,128)S(1)}, u32[]{:S(2)}) copy-start(f32[16,256]{1,0:T(8,128)S(1)} %get-tuple-element.102) | copy-start | bytes 49156
  322.9 13.1 %copy-start.3 = (f32[2,8,3,256]{3,2,1,0:T(4,128)S(1)}, f32[2,8,3,256]{3,2,1,0:T(4,128)}, u32[]{:S(2)}) copy-start(f32[2,8,3,256]{3,2,1,0:T(4,128)} %copy-done.2) | copy-start | bytes 147460
where the time goes:
time: 378 us; the launch traced here: 377 us
  blocking collectives  249 us (66%)
  matrix products  94.6 us (25%)
  local copies, waits for them, and re-layouts  18.1 us (5%)
  other arithmetic  10.5 us (3%)
    dot_general x4, matrix products, near_block(): jnp.einsum('bkij,bkj->bi', coupling, weights, precision=HIGHEST_PRECISION)  79 us
    unnamed x2, blocking collectives  78.8 us
    psum x1, blocking collectives, per_device(): squares_start = lax.psum(jnp.sum(start * start), ('group', 'dev'))  42.2 us
    psum x1, blocking collectives, per_device(): lax.psum(jnp.sum(orthogonal * orthogonal), ('group', 'dev'))  41.1 us
    psum x1, blocking collectives, per_device(): lax.psum((jnp.sum(unit_first * product_first), jnp.sum(unit_first * unit_...  38.7 us
    all_gather x2, blocking collectives, fetch(): lax.all_gather(flat_moments, 'dev', axis=0, tiled=True)  20.6 us
    all_gather x2, blocking collectives, fetch(): lax.all_gather(charges, 'dev', axis=0, tiled=True)  19.2 us
    all_gather x1, blocking collectives, per_device(): every_point = lax.all_gather(coords, 'dev', axis=0, tiled=True)  8.84 us

commit v1 on v0

v1 whole, which is shorter than its diff:
```python
import functools
import math

import jax
import jax.numpy as jnp
from jax import lax
from jax.experimental import pallas as pl
from jax.experimental.pallas import tpu as pltpu
from jax.sharding import PartitionSpec as P

FOUR_PI = 4.0 * math.pi
SOFTENING = 0.01
EPSILON = 1e-06
LIFT = 1024.0
MESH = pl.DeviceIdType.MESH
LANES = 128


def thirds(x):
    high = x.astype(jnp.bfloat16).astype(jnp.float32)
    rest = x - high
    middle = rest.astype(jnp.bfloat16).astype(jnp.float32)
    return high, middle, rest - middle


def kernel(
    devs, groups, near_ref, far_ref, top_ref, start_ref, coords_ref, area_ref, basis_ref,
    couple_ref, transfer_ref, ctop_ref, out1_ref, out2_ref, points, weights, weights2, moms,
    moms2, tops, tops2, norms, kmat, near_acc, down_ref, send_sem, recv_sem, xsend_sem, xrecv_sem,
):
    leaves, panels = start_ref.shape
    entries = near_ref.shape[1]
    coeffs = basis_ref.shape[1]
    fars = far_ref.shape[1]
    pairs = leaves // 2
    me = lax.axis_index("dev")
    grp = lax.axis_index("group")
    base = me * leaves

    def dev_peer(k):
        return (grp, lax.rem(me + k, devs))

    def grp_peer(k):
        return (lax.rem(grp + k, groups), me)

    barrier = pltpu.get_barrier_semaphore()

    def greet_dev(k, c):
        pl.semaphore_signal(barrier, inc=1, device_id=dev_peer(k), device_id_type=MESH)
        return c

    def greet_grp(k, c):
        pl.semaphore_signal(barrier, inc=1, device_id=grp_peer(k), device_id_type=MESH)
        return c

    lax.fori_loop(1, devs, greet_dev, 0)
    lax.fori_loop(1, groups, greet_grp, 0)
    pl.semaphore_wait(barrier, devs + groups - 2)

    def copy_in_group(phase, buf, first, rows, k):
        part = buf.at[pl.ds(first, rows)]
        return pltpu.make_async_remote_copy(
            src_ref=part, dst_ref=part, send_sem=send_sem.at[phase, k],
            recv_sem=recv_sem.at[phase, k], device_id=dev_peer(k), device_id_type=MESH,
        )

    def copy_across(phase, buf, k):
        part = buf.at[pl.ds(grp * devs, devs)]
        return pltpu.make_async_remote_copy(
            src_ref=part, dst_ref=part, send_sem=xsend_sem.at[phase, k],
            recv_sem=xrecv_sem.at[phase, k], device_id=grp_peer(k), device_id_type=MESH,
        )

    def in_group(phase, buf, per_dev, offset=0):
        first = offset + me * per_dev

        def start(k, c):
            copy_in_group(phase, buf, first, per_dev, k).start()
            return c

        def arrive(k, c):
            sender = lax.rem(me - k + devs, devs)
            copy_in_group(phase, buf, offset + sender * per_dev, per_dev, k).wait_recv()
            return c

        def sent(k, c):
            copy_in_group(phase, buf, first, per_dev, k).wait_send()
            return c

        return tuple(
            functools.partial(lax.fori_loop, 1, devs, f, 0) for f in (start, arrive, sent)
        )

    def across(phase, buf):
        def start(k, c):
            copy_across(phase, buf, k).start()
            return c

        def arrive(k, c):
            sender = lax.rem(grp - k + groups, groups)
            part = buf.at[pl.ds(sender * devs, devs)]
            pltpu.make_async_remote_copy(
                src_ref=part, dst_ref=part, send_sem=xsend_sem.at[phase, k],
                recv_sem=xrecv_sem.at[phase, k], device_id=grp_peer(k), device_id_type=MESH,
            ).wait_recv()
            return c

        def sent(k, c):
            copy_across(phase, buf, k).wait_send()
            return c

        return tuple(
            functools.partial(lax.fori_loop, 1, groups, f, 0) for f in (start, arrive, sent)
        )

    points_c = in_group(0, points, 3 * leaves)
    weights_c = in_group(1, weights, leaves)
    moms_c = in_group(2, moms, leaves)
    tops_c = in_group(3, tops, 1, grp * devs)
    weights2_c = in_group(4, weights2, leaves)
    moms2_c = in_group(5, moms2, leaves)
    tops2_c = in_group(6, tops2, 1, grp * devs)
    norms_c = in_group(7, norms, 1, grp * devs)
    tops_x = across(0, tops)
    tops2_x = across(1, tops2)
    norms_x = across(2, norms)

    lane = lax.broadcasted_iota(jnp.int32, (1, LANES), 1)
    low_half = lane < coeffs
    row_r = lax.broadcasted_iota(jnp.int32, (coeffs, LANES), 0)
    lane_r = lax.broadcasted_iota(jnp.int32, (coeffs, LANES), 1)
    twice_eye = lax.rem(lane_r, coeffs) == row_r
    row_p = lax.broadcasted_iota(jnp.int32, (LANES, LANES), 0)
    lane_p = lax.broadcasted_iota(jnp.int32, (LANES, LANES), 1)
    eye = row_p == lane_p
    row8 = lax.broadcasted_iota(jnp.int32, (8, panels), 0)

    def lane_sum(x):
        total = x[:, :LANES]
        for j in range(1, x.shape[1] // LANES):
            total = total + x[:, j * LANES:(j + 1) * LANES]
        return jnp.sum(total, axis=1, keepdims=True)

    def total_of(x):
        return jnp.sum(jnp.sum(x, axis=0, keepdims=True), axis=1, keepdims=True)

    def twice_row(column):
        return jnp.sum(jnp.where(twice_eye, column, 0.0), axis=0, keepdims=True)

    def find_moments(charges, table):
        def body(l, c):
            product = basis_ref[l] * charges[pl.ds(base + l, 1), :]
            table[pl.ds(base + l, 1), :] = twice_row(lane_sum(product))
            return c

        lax.fori_loop(0, leaves, body, 0)

    def find_cluster(table):
        total = jnp.zeros((coeffs, LANES), jnp.float32)
        for j in range(pairs):
            pair = jnp.where(
                low_half, table[pl.ds(base + 2 * j, 1), :], table[pl.ds(base + 2 * j + 1, 1), :]
            )
            total = total + transfer_ref[0, :, j * LANES:(j + 1) * LANES] * pair
        return twice_row(lane_sum(total))

    def find_down(clusters):
        total = jnp.zeros((coeffs, LANES), jnp.float32)
        for j in range(top_ref.shape[1] // 2):
            pair = jnp.where(
                low_half, clusters[top_ref[0, 2 * j]],
                pltpu.roll(clusters[top_ref[0, 2 * j + 1]], coeffs, 1),
            )
            total = total + ctop_ref[0, :, j * LANES:(j + 1) * LANES] * pair
        level = lane_sum(total)
        for j in range(pairs):
            down_ref[j:j + 1, :] = jnp.sum(
                transfer_ref[0, :, j * LANES:(j + 1) * LANES] * level, axis=0, keepdims=True
            )

    def far_row(l, table):
        half = lax.rem(l, 2) * coeffs
        total = jnp.where(lane_r == row_r + half, down_ref[pl.ds(l // 2, 1), :], 0.0)
        for j in range(fars // 2):
            pair = jnp.where(
                low_half, table[pl.ds(far_ref[l, 2 * j], 1), :],
                table[pl.ds(far_ref[l, 2 * j + 1], 1), :],
            )
            total = total + couple_ref[l, :, j * LANES:(j + 1) * LANES] * pair
        return jnp.sum(basis_ref[l] * lane_sum(total), axis=0, keepdims=True)

    def source_of(l, n):
        named = near_ref[l, n]
        live = named >= 0
        index = jnp.where(live, named - grp * (devs * leaves), base + l)
        index = jnp.clip(index, 0, devs * leaves - 1)
        return index, jnp.where(live, 1.0 / FOUR_PI, 0.0)

    def point_rows(index):
        return [points[pl.ds(3 * index + c, 1), :] for c in range(3)]

    def stack8(rows):
        total = jnp.zeros((8, panels), jnp.float32)
        for c, row in enumerate(rows):
            total = jnp.where(row8 == c, row, total)
        return total

    def to_row(acc):
        column = jnp.sum(acc, axis=1, keepdims=True)
        parts = [
            jnp.sum(
                jnp.where(eye, column[h * LANES:(h + 1) * LANES], 0.0), axis=0, keepdims=True
            )
            for h in range(panels // LANES)
        ]
        return jnp.concatenate(parts, axis=1)

    def take_points(l, c):
        for axis in range(3):
            points[pl.ds(3 * (base + l) + axis, 1), :] = coords_ref[l, axis:axis + 1, :]
        return c

    lax.fori_loop(0, leaves, take_points, 0)
    points_c[0]()
    weights[pl.ds(base, leaves), :] = area_ref[...] * (start_ref[...] * LIFT)
    weights_c[0]()
    find_moments(weights, moms)
    moms_c[0]()
    squares = total_of(start_ref[...] * start_ref[...])
    tops[grp * devs + me] = jnp.where(low_half, find_cluster(moms), squares)
    tops_c[0]()
    points_c[1]()
    weights_c[1]()
    tops_c[1]()
    tops_x[0]()

    def near_first(l, c):
        x, y, z = point_rows(base + l)
        size = x * x + y * y + z * z + SOFTENING
        high, middle, low = thirds(
            stack8((-2.0 * x, -2.0 * y, -2.0 * z, size, jnp.ones_like(x)))
        )
        targets = jnp.concatenate((high, high, middle, middle, high, low), axis=0)
        targets = jnp.transpose(targets).astype(jnp.bfloat16)
        acc = jnp.zeros((panels, LANES), jnp.float32)
        for n in range(entries):
            index, scale = source_of(l, n)
            x, y, z = point_rows(index)
            high, middle, low = thirds(
                stack8((x, y, z, jnp.ones_like(x), x * x + y * y + z * z))
            )
            sources = jnp.concatenate((high, middle, high, middle, low, high), axis=0)
            squared = jnp.dot(
                targets, sources.astype(jnp.bfloat16), preferred_element_type=jnp.float32
            )
            coupling = lax.rsqrt(squared)
            kmat[l * entries + n] = coupling
            row = weights[pl.ds(index, 1), :] * scale
            for h in range(panels // LANES):
                cut = slice(h * LANES, (h + 1) * LANES)
                acc = acc + coupling[:, cut] * row[:, cut]
        near_acc[pl.ds(l, 1), :] = to_row(acc)
        return c

    lax.fori_loop(0, leaves, near_first, 0)
    moms_c[1]()
    tops_x[1]()
    find_down(tops)

    panels_all = float(leaves * panels * devs * groups)

    def scale_of(total):
        return 1.0 / jnp.sqrt(total / panels_all + EPSILON)

    def pick(row, at):
        return jnp.sum(jnp.where(lane == at, row, 0.0), axis=1, keepdims=True)

    first_scale = scale_of(pick(jnp.sum(tops[...], axis=0), coeffs))

    def far_first(l, c):
        near_acc[pl.ds(l, 1), :] = near_acc[pl.ds(l, 1), :] + far_row(l, moms)
        return c

    lax.fori_loop(0, leaves, far_first, 0)
    product = near_acc[...] * (first_scale * (1.0 / LIFT))
    unit = start_ref[...] * first_scale
    out1_ref[...] = product
    weights2[pl.ds(base, leaves), :] = area_ref[...] * product
    weights2_c[0]()
    find_moments(weights2, moms2)
    moms2_c[0]()
    along = total_of(unit * product)
    length = total_of(unit * unit)
    sums = jnp.where(lane < coeffs + coeffs // 2, along, length)
    tops2[grp * devs + me] = jnp.where(low_half, find_cluster(moms2), sums)
    tops2_c[0]()
    weights2_c[1]()
    tops2_c[1]()
    tops2_x[0]()

    def near_second(l, c):
        acc = jnp.zeros((panels, LANES), jnp.float32)
        for n in range(entries):
            index, scale = source_of(l, n)
            row = weights2[pl.ds(index, 1), :] * scale
            for h in range(panels // LANES):
                cut = slice(h * LANES, (h + 1) * LANES)
                acc = acc + kmat[l * entries + n, :, cut] * row[:, cut]
        near_acc[pl.ds(l, 1), :] = to_row(acc)
        return c

    some = leaves // 2
    lax.fori_loop(0, some, near_second, 0)
    tops2_x[1]()
    sums = jnp.sum(tops2[...], axis=0)
    projection = pick(sums, coeffs) / pick(sums, coeffs + coeffs // 2)
    product = out1_ref[...]
    orthogonal = product - projection * (start_ref[...] * first_scale)
    norms[grp * devs + me] = jnp.broadcast_to(total_of(orthogonal * orthogonal), (1, LANES))
    norms_c[0]()
    lax.fori_loop(some, leaves, near_second, 0)
    norms_c[1]()
    norms_x[0]()
    moms2_c[1]()
    find_down(tops2)

    def far_second(l, c):
        near_acc[pl.ds(l, 1), :] = near_acc[pl.ds(l, 1), :] + far_row(l, moms2)
        return c

    lax.fori_loop(0, leaves, far_second, 0)
    norms_x[1]()
    second_scale = scale_of(pick(jnp.sum(norms[...], axis=0), 0))
    out2_ref[...] = (near_acc[...] - projection * out1_ref[...]) * second_scale

    for copies in (
        points_c, weights_c, moms_c, tops_c, weights2_c, moms2_c, tops2_c, norms_c,
        tops_x, tops2_x, norms_x,
    ):
        copies[2]()


def per_device(
    start, coords, area, near_list, basis, far_leaf, couple_leaf, transfer, far_top, couple_top
):
    leaves, panels = start.shape
    entries = near_list.shape[1]
    devs = lax.axis_size("dev")
    groups = lax.axis_size("group")
    smem = pl.BlockSpec(memory_space=pltpu.SMEM)
    vmem = pl.BlockSpec(memory_space=pltpu.VMEM)
    f32 = jnp.float32
    return tuple(pl.pallas_call(
        functools.partial(kernel, devs, groups),
        out_shape=[jax.ShapeDtypeStruct((leaves, panels), f32)] * 2,
        in_specs=[smem] * 3 + [vmem] * 7,
        out_specs=[vmem] * 2,
        scratch_shapes=[
            pltpu.VMEM((devs * leaves * 3, panels), f32),
            pltpu.VMEM((devs * leaves, panels), f32),
            pltpu.VMEM((devs * leaves, panels), f32),
            pltpu.VMEM((devs * leaves, LANES), f32),
            pltpu.VMEM((devs * leaves, LANES), f32),
            pltpu.VMEM((groups * devs, 1, LANES), f32),
            pltpu.VMEM((groups * devs, 1, LANES), f32),
            pltpu.VMEM((groups * devs, 1, LANES), f32),
            pltpu.VMEM((leaves * entries, panels, panels), f32),
            pltpu.VMEM((leaves, panels), f32),
            pltpu.VMEM((leaves // 2, LANES), f32),
            pltpu.SemaphoreType.DMA((8, devs)),
            pltpu.SemaphoreType.DMA((8, devs)),
            pltpu.SemaphoreType.DMA((3, groups)),
            pltpu.SemaphoreType.DMA((3, groups)),
        ],
        compiler_params=pltpu.CompilerParams(
            collective_id=0, has_side_effects=True, vmem_limit_bytes=48 * 1024 * 1024
        ),
    )(near_list, far_leaf, far_top, start, coords, area, basis, couple_leaf, transfer, couple_top))


def solution(mesh):
    rows = P(("group", "dev"), None)
    blocks = P(("group", "dev"), None, None)
    in_specs = (rows, blocks, rows, rows, blocks, rows, blocks, blocks, rows, blocks)
    return jax.shard_map(
        per_device, mesh=mesh, in_specs=in_specs, out_specs=(rows, rows), check_vma=False
    )
```

time: 378 us -> 54.4 us (0.14)
  blocking collectives: 249 us -> 0 us
  matrix products: 94.6 us -> 0 us
  Pallas kernels: 0 us -> 42.9 us
  other arithmetic: 10.5 us -> 0 us
  local copies, waits for them, and re-layouts: 18.1 us -> 10.4 us
    psum x3 -> x0, blocking collectives: 122 us -> none  [the longest x1 42.2 us: per_device(): squares_start = lax.psum(jnp.sum(start * start), ('group', 'dev'))]
    dot_general x16 -> x0, matrix products: 94.6 us -> none  [the longest x4 79 us: near_block(): jnp.einsum('bkij,bkj->bi', coupling, weights, precision=HIGHEST_PRECISION)]
    unnamed x2 -> x0, blocking collectives: 78.8 us -> none
    all_gather x5 -> x0, blocking collectives: 48.6 us -> none  [the longest x2 20.6 us: fetch(): lax.all_gather(flat_moments, 'dev', axis=0, tiled=True)]
    pallas_call x0 -> x1, Pallas kernels: none -> 42.9 us  [per_device(): pl.pallas_call(functools.partial(kernel, devs, groups), out_shape=[jax.Sh...]
    unnamed x29 -> x19, local copies, waits for them, and re-layouts: 1.96 us -> 10.4 us
    gather x9 -> x0, local copies, waits for them, and re-layouts: 5.94 us -> none  [the longest x2 2.46 us: far_finish(): partners = moment_table[far_leaf].reshape(leaves, -1)]
    reshape x4 -> x0, local copies, waits for them, and re-layouts: 4.15 us -> none  [the longest x2 2.48 us: far_finish(): partners = moment_table[far_leaf].reshape(leaves, -1)]
where the time goes in v1:
time: 54.4 us; the launch traced here: 53.9 us
  Pallas kernels  42.9 us (79%)
  local copies, waits for them, and re-layouts  10.4 us (19%)
  between operations  0.66 us (1%)
    pallas_call x1, Pallas kernels, per_device(): pl.pallas_call(functools.partial(kernel, devs, groups), out_shape=[jax.Sh...  42.9 us
    unnamed x19, local copies, waits for them, and re-layouts  10.4 us

profile of v1, /device:TPU:0, one launch (start us, length us, event | category | flops | bytes accessed | tf_op | source)
XLA Modules:
  0.0 53.9 jit_solution(16938048545827434293)
XLA Ops:
  0.6 0.8 %copy.12.near_ref = s32[16,6]{1,0:T(8,128)S(1)} copy(s32[16,6]{0,1:T(8,128)} %param.13) | data formatting | bytes 768 | tf_op args[3]
  1.4 0.8 %copy.13.far_ref = s32[16,8]{1,0:T(8,128)S(1)} copy(s32[16,8]{0,1:T(8,128)} %param.15) | data formatting | bytes 1024 | tf_op args[5]
  2.2 0.8 %copy.14.coords_ref = f32[16,3,256]{2,1,0:T(4,128)S(1)} copy(f32[16,3,256]{2,0,1:T(8,128)} %param.11) | data formatting | bytes 98304 | tf_op args[1]
  3.0 0.0 copy-start
  3.0 1.6 %copy-done = f32[16,64,512]{2,1,0:T(8,128)S(1)} copy-done((f32[16,64,512]{2,1,0:T(8,128)S(1)}, f32[16,64,512]{2,1,0:T(8,128)}, u32[]{:S(2)}) %copy-start) | copy-done | bytes 2097176
  4.6 0.0 copy-start.1
  4.6 1.2 %copy-done.1 = f32[16,64,256]{2,1,0:T(8,128)S(1)} copy-done((f32[16,64,256]{2,1,0:T(8,128)S(1)}, f32[16,64,256]{2,1,0:T(8,128)}, u32[]{:S(2)}) %copy-start.1) | copy-done | bytes 1048600
  5.8 0.0 copy-start.2
  5.8 0.9 %copy-done.2 = f32[1,64,1024]{2,1,0:T(8,128)S(1)} copy-done((f32[1,64,1024]{2,1,0:T(8,128)S(1)}, f32[1,64,1024]{2,1,0:T(8,128)}, u32[]{:S(2)}) %copy-start.2) | copy-done | bytes 262168
  6.8 0.0 copy-start.3
  6.8 0.9 %copy-done.3 = f32[1,64,1024]{2,1,0:T(8,128)S(1)} copy-done((f32[1,64,1024]{2,1,0:T(8,128)S(1)}, f32[1,64,1024]{2,1,0:T(8,128)}, u32[]{:S(2)}) %copy-start.3) | copy-done | bytes 262168
  7.7 0.0 copy-start.4
  7.7 0.7 %copy-done.4 = f32[16,256]{1,0:T(8,128)S(1)} copy-done((f32[16,256]{1,0:T(8,128)S(1)}, f32[16,256]{1,0:T(8,128)}, u32[]{:S(2)}) %copy-start.4) | copy-done | bytes 16408
  8.4 0.0 copy-start.5
  8.4 0.7 %copy-done.5 = f32[16,256]{1,0:T(8,128)S(1)} copy-done((f32[16,256]{1,0:T(8,128)S(1)}, f32[16,256]{1,0:T(8,128)}, u32[]{:S(2)}) %copy-start.5) | copy-done | bytes 16408
  9.1 0.0 copy-start.6
  9.1 0.7 %copy-done.6 = s32[1,16]{1,0:T(1,128)S(1)} copy-done((s32[1,16]{1,0:T(1,128)S(1)}, s32[1,16]{1,0:T(1,128)}, u32[]{:S(2)}) %copy-start.6) | copy-done | bytes 88
  9.8 42.9 %shard_map.113 = (f32[16,256]{1,0:T(8,128)S(1)}, f32[16,256]{1,0:T(8,128)S(1)}) custom-call(s32[16,6]{1,0:T(8,128)S(1)} %copy.12.near_ref, s32[16,8]{1,0:T(8,128)S(1)} %copy.13.far_ref, s32[1,16]{1,0:T(1,128)S(1)} %copy-done.6, f32[16,256]{1,0:T(8,128)S(1)} %copy-done.4, f32[16,3,256]{2,1,0:T(4,128)S(1)} %copy.14.coords_ref, f32[16,256]{1,0:T(8,128)S(1)} %copy-done.5, ...), custom_call_target="tpu_custom_call" | custom-call | tf_op jit(solution)/shard_map/pallas_call | solution.py:353
  52.7 0.6 %copy.17 = f32[16,256]{1,0:T(8,128)} copy(f32[16,256]{1,0:T(8,128)S(1)} %get-tuple-element.4) | data formatting | bytes 32768
  53.3 0.6 %copy.18 = f32[16,256]{1,0:T(8,128)} copy(f32[16,256]{1,0:T(8,128)S(1)} %get-tuple-element.5) | data formatting | bytes 32768
Async XLA Ops:
  3.0 1.6 %copy-start = (f32[16,64,512]{2,1,0:T(8,128)S(1)}, f32[16,64,512]{2,1,0:T(8,128)}, u32[]{:S(2)}) copy-start(f32[16,64,512]{2,1,0:T(8,128)} %couple_ref.1) | copy-start | bytes 6291460
  4.6 1.2 %copy-start.1 = (f32[16,64,256]{2,1,0:T(8,128)S(1)}, f32[16,64,256]{2,1,0:T(8,128)}, u32[]{:S(2)}) copy-start(f32[16,64,256]{2,1,0:T(8,128)} %basis_ref.1) | copy-start | bytes 3145732
  5.8 0.9 %copy-start.2 = (f32[1,64,1024]{2,1,0:T(8,128)S(1)}, f32[1,64,1024]{2,1,0:T(8,128)}, u32[]{:S(2)}) copy-start(f32[1,64,1024]{2,1,0:T(8,128)} %transfer_ref.1) | copy-start | bytes 786436
  6.8 0.9 %copy-start.3 = (f32[1,64,1024]{2,1,0:T(8,128)S(1)}, f32[1,64,1024]{2,1,0:T(8,128)}, u32[]{:S(2)}) copy-start(f32[1,64,1024]{2,1,0:T(8,128)} %ctop_ref.1) | copy-start | bytes 786436
  7.7 0.7 %copy-start.4 = (f32[16,256]{1,0:T(8,128)S(1)}, f32[16,256]{1,0:T(8,128)}, u32[]{:S(2)}) copy-start(f32[16,256]{1,0:T(8,128)} %start_ref.1) | copy-start | bytes 49156
  8.4 0.7 %copy-start.5 = (f32[16,256]{1,0:T(8,128)S(1)}, f32[16,256]{1,0:T(8,128)}, u32[]{:S(2)}) copy-start(f32[16,256]{1,0:T(8,128)} %area_ref.1) | copy-start | bytes 49156
  9.1 0.7 %copy-start.6 = (s32[1,16]{1,0:T(1,128)S(1)}, s32[1,16]{1,0:T(1,128)}, u32[]{:S(2)}) copy-start(s32[1,16]{1,0:T(1,128)} %top_ref.1) | copy-start | bytes 196

commit v2 on v1

v2 whole, which is shorter than its diff:
```python
import functools
import math

import jax
import jax.numpy as jnp
from jax import lax
from jax.experimental import pallas as pl
from jax.experimental.pallas import tpu as pltpu
from jax.sharding import PartitionSpec as P

FOUR_PI = 4.0 * math.pi
SOFTENING = 0.01
EPSILON = 1e-06
LIFT = 1024.0
MESH = pl.DeviceIdType.MESH
LANES = 128


def thirds(x):
    high = x.astype(jnp.bfloat16).astype(jnp.float32)
    rest = x - high
    middle = rest.astype(jnp.bfloat16).astype(jnp.float32)
    return high, middle, rest - middle


def kernel(
    devs, groups, near_ref, far_ref, top_ref, start_hbm, coords_hbm, area_hbm, basis_hbm,
    couple_hbm, transfer_hbm, ctop_hbm, out_ref, start_ref, area_ref, basis_ref, couple_ref,
    transfer_ref, ctop_ref, points, parcel, parcel2, tops, tops2, kmat, near_acc, down_ref,
    load_sem, send_sem, recv_sem, xsend_sem, xrecv_sem,
):
    leaves, panels = start_ref.shape
    entries = near_ref.shape[0]
    coeffs = basis_ref.shape[1]
    fars = far_ref.shape[0]
    pairs = leaves // 2
    halves = panels // LANES
    mom_row = halves * leaves
    top_row = mom_row + leaves
    me = lax.axis_index("dev")
    grp = lax.axis_index("group")

    def dev_peer(k):
        return (grp, lax.rem(me + k, devs))

    def grp_peer(k):
        return (lax.rem(grp + k, groups), me)

    barrier = pltpu.get_barrier_semaphore()

    def greet_dev(k, c):
        pl.semaphore_signal(barrier, inc=1, device_id=dev_peer(k), device_id_type=MESH)
        return c

    def greet_grp(k, c):
        pl.semaphore_signal(barrier, inc=1, device_id=grp_peer(k), device_id_type=MESH)
        return c

    lax.fori_loop(1, devs, greet_dev, 0)
    lax.fori_loop(1, groups, greet_grp, 0)

    loads = [
        pltpu.make_async_copy(source, target, load_sem.at[n])
        for n, (source, target) in enumerate((
            (start_hbm, start_ref), (area_hbm, area_ref), (basis_hbm, basis_ref),
            (transfer_hbm, transfer_ref), (coords_hbm, points.at[me]), (ctop_hbm, ctop_ref),
            (couple_hbm, couple_ref),
        ))
    ]
    for load in loads:
        load.start()

    def in_group(phase, buf, first):
        def copy(source, block, k):
            return pltpu.make_async_remote_copy(
                src_ref=source, dst_ref=buf.at[block], send_sem=send_sem.at[phase, k],
                recv_sem=recv_sem.at[phase, k], device_id=dev_peer(k), device_id_type=MESH,
            )

        def start(k, c):
            copy(first, me, k).start()
            return c

        def arrive(k, c):
            sender = lax.rem(me - k + devs, devs)
            copy(buf.at[sender], sender, k).wait_recv()
            return c

        def sent(k, c):
            copy(first, me, k).wait_send()
            return c

        return tuple(
            functools.partial(lax.fori_loop, 1, devs, f, 0) for f in (start, arrive, sent)
        )

    def across(phase, buf):
        def copy(block, k):
            part = buf.at[pl.ds(block * devs, devs)]
            return pltpu.make_async_remote_copy(
                src_ref=part, dst_ref=part, send_sem=xsend_sem.at[phase, k],
                recv_sem=xrecv_sem.at[phase, k], device_id=grp_peer(k), device_id_type=MESH,
            )

        def start(k, c):
            copy(grp, k).start()
            return c

        def arrive(k, c):
            copy(lax.rem(grp - k + groups, groups), k).wait_recv()
            return c

        def sent(k, c):
            copy(grp, k).wait_send()
            return c

        return tuple(
            functools.partial(lax.fori_loop, 1, groups, f, 0) for f in (start, arrive, sent)
        )

    points_c = in_group(0, points, coords_hbm)
    parcel_c = in_group(1, parcel, parcel.at[me])
    parcel2_c = in_group(2, parcel2, parcel2.at[me])
    tops_x = across(0, tops)
    tops2_x = across(1, tops2)

    lane = lax.broadcasted_iota(jnp.int32, (1, LANES), 1)
    low_half = lane < coeffs
    row_r = lax.broadcasted_iota(jnp.int32, (coeffs, LANES), 0)
    lane_r = lax.broadcasted_iota(jnp.int32, (coeffs, LANES), 1)
    twice_eye = lax.rem(lane_r, coeffs) == row_r
    row_p = lax.broadcasted_iota(jnp.int32, (LANES, LANES), 0)
    lane_p = lax.broadcasted_iota(jnp.int32, (LANES, LANES), 1)
    eye = row_p == lane_p
    row8 = lax.broadcasted_iota(jnp.int32, (8, panels), 0)

    def lane_sum(x):
        total = x[:, :LANES]
        for j in range(1, x.shape[1] // LANES):
            total = total + x[:, j * LANES:(j + 1) * LANES]
        return jnp.sum(total, axis=1, keepdims=True)

    def total_of(x):
        return jnp.sum(jnp.sum(x, axis=0, keepdims=True), axis=1, keepdims=True)

    def twice_row(column):
        return jnp.sum(jnp.where(twice_eye, column, 0.0), axis=0, keepdims=True)

    def moment_row(table, index):
        return table[index // leaves, pl.ds(mom_row + lax.rem(index, leaves), 1), :]

    def pack(table, charges, sums):
        for h in range(halves):
            table[me, h * leaves:(h + 1) * leaves, :] = charges[:, h * LANES:(h + 1) * LANES]

        def body(l, c):
            total = jnp.zeros((coeffs, LANES), jnp.float32)
            for h in range(halves):
                row = table[me, pl.ds(h * leaves + l, 1), :]
                total = total + basis_ref[l, :, h * LANES:(h + 1) * LANES] * row
            table[me, pl.ds(mom_row + l, 1), :] = twice_row(lane_sum(total))
            return c

        lax.fori_loop(0, leaves, body, 0)
        total = jnp.zeros((coeffs, LANES), jnp.float32)
        for j in range(pairs):
            row = mom_row + 2 * j
            pair = jnp.where(low_half, table[me, row:row + 1, :], table[me, row + 1:row + 2, :])
            total = total + transfer_ref[0, :, j * LANES:(j + 1) * LANES] * pair
        cluster = jnp.where(low_half, twice_row(lane_sum(total)), sums)
        table[me, top_row:top_row + 8, :] = jnp.broadcast_to(cluster, (8, LANES))

    def collect_tops(table, clusters):
        def body(d, c):
            clusters[grp * devs + d] = table[d, top_row:top_row + 1, :]
            return c

        lax.fori_loop(0, devs, body, 0)

    def find_down(clusters):
        total = jnp.zeros((coeffs, LANES), jnp.float32)
        for j in range(top_ref.shape[1] // 2):
            pair = jnp.where(
                low_half, clusters[top_ref[0, 2 * j]],
                pltpu.roll(clusters[top_ref[0, 2 * j + 1]], coeffs, 1),
            )
            total = total + ctop_ref[0, :, j * LANES:(j + 1) * LANES] * pair
        level = lane_sum(total)
        for j in range(pairs):
            down_ref[j:j + 1, :] = jnp.sum(
                transfer_ref[0, :, j * LANES:(j + 1) * LANES] * level, axis=0, keepdims=True
            )

    def far_row(l, table):
        half = lax.rem(l, 2) * coeffs
        total = jnp.where(lane_r == row_r + half, down_ref[pl.ds(l // 2, 1), :], 0.0)
        for j in range(fars // 2):
            pair = jnp.where(
                low_half, moment_row(table, far_ref[2 * j, l]), moment_row(table, far_ref[2 * j + 1, l])
            )
            total = total + couple_ref[l, :, j * LANES:(j + 1) * LANES] * pair
        return jnp.sum(basis_ref[l] * lane_sum(total), axis=0, keepdims=True)

    def source_of(l, n):
        named = near_ref[n, l]
        live = named >= 0
        index = jnp.where(live, named - grp * (devs * leaves), me * leaves + l)
        index = jnp.clip(index, 0, devs * leaves - 1)
        return index, jnp.where(live, 1.0 / FOUR_PI, 0.0)

    def point_rows(index):
        device, leaf = index // leaves, lax.rem(index, leaves)
        return [points[device, c, pl.ds(leaf, 1), :] for c in range(3)]

    def charge_rows(table, index, scale):
        device, leaf = index // leaves, lax.rem(index, leaves)
        return [
            table[device, pl.ds(h * leaves + leaf, 1), :] * scale for h in range(halves)
        ]

    def stack8(rows):
        total = jnp.zeros((8, panels), jnp.float32)
        for c, row in enumerate(rows):
            total = jnp.where(row8 == c, row, total)
        return total

    def to_row(acc):
        column = jnp.sum(acc, axis=1, keepdims=True)
        parts = [
            jnp.sum(
                jnp.where(eye, column[h * LANES:(h + 1) * LANES], 0.0), axis=0, keepdims=True
            )
            for h in range(panels // LANES)
        ]
        return jnp.concatenate(parts, axis=1)

    loads[0].wait()
    loads[1].wait()
    squares = total_of(start_ref[...] * start_ref[...])
    pl.semaphore_wait(barrier, devs + groups - 2)
    points_c[0]()
    loads[2].wait()
    loads[3].wait()
    pack(parcel, area_ref[...] * (start_ref[...] * LIFT), squares)
    parcel_c[0]()
    loads[4].wait()
    points_c[1]()
    parcel_c[1]()
    collect_tops(parcel, tops)
    tops_x[0]()

    def near_first(l, c):
        x, y, z = point_rows(me * leaves + l)
        size = x * x + y * y + z * z + SOFTENING
        high, middle, low = thirds(
            stack8((-2.0 * x, -2.0 * y, -2.0 * z, size, jnp.ones_like(x)))
        )
        targets = jnp.concatenate((high, high, middle, middle, high, low), axis=0)
        targets = jnp.transpose(targets).astype(jnp.bfloat16)
        acc = jnp.zeros((panels, LANES), jnp.float32)
        for n in range(entries):
            index, scale = source_of(l, n)
            x, y, z = point_rows(index)
            high, middle, low = thirds(
                stack8((x, y, z, jnp.ones_like(x), x * x + y * y + z * z))
            )
            sources = jnp.concatenate((high, middle, high, middle, low, high), axis=0)
            squared = jnp.dot(
                targets, sources.astype(jnp.bfloat16), preferred_element_type=jnp.float32
            )
            coupling = lax.rsqrt(squared)
            kmat[l * entries + n] = coupling
            for h, row in enumerate(charge_rows(parcel, index, scale)):
                acc = acc + coupling[:, h * LANES:(h + 1) * LANES] * row
        near_acc[pl.ds(l, 1), :] = to_row(acc)
        return c

    lax.fori_loop(0, leaves, near_first, 0)
    tops_x[1]()
    loads[5].wait()
    loads[6].wait()
    find_down(tops)

    panels_all = float(leaves * panels * devs * groups)

    def scale_of(total):
        return 1.0 / jnp.sqrt(total / panels_all + EPSILON)

    def pick(row, at):
        return jnp.sum(jnp.where(lane == at, row, 0.0), axis=1, keepdims=True)

    first_scale = scale_of(pick(jnp.sum(tops[...], axis=0), coeffs))

    def far_first(l, c):
        near_acc[pl.ds(l, 1), :] = near_acc[pl.ds(l, 1), :] + far_row(l, parcel)
        return c

    lax.fori_loop(0, leaves, far_first, 0)
    product = near_acc[...] * (first_scale * (1.0 / LIFT))
    unit = start_ref[...] * first_scale
    out_ref[0] = product
    along = total_of(unit * product)
    length = total_of(unit * unit)
    part = jnp.where(length > 0.0, along / length, 0.0)
    beyond = total_of((product - part * unit) ** 2)
    sums = jnp.where(
        lane == coeffs, along, jnp.where(lane == coeffs + 1, length, jnp.where(
            lane == coeffs + 2, beyond, part
        ))
    )
    pack(parcel2, area_ref[...] * product, sums)
    parcel2_c[0]()
    parcel2_c[1]()
    collect_tops(parcel2, tops2)
    tops2_x[0]()

    def near_second(l, c):
        acc = jnp.zeros((panels, LANES), jnp.float32)
        for n in range(entries):
            index, scale = source_of(l, n)
            for h, row in enumerate(charge_rows(parcel2, index, scale)):
                acc = acc + kmat[l * entries + n, :, h * LANES:(h + 1) * LANES] * row
        near_acc[pl.ds(l, 1), :] = to_row(acc)
        return c

    lax.fori_loop(0, leaves, near_second, 0)
    tops2_x[1]()
    find_down(tops2)
    rows = tops2[...].reshape(groups * devs, LANES)

    def column(at):
        return jnp.sum(jnp.where(lane == at, rows, 0.0), axis=1, keepdims=True)

    lengths = column(coeffs + 1)
    projection = total_of(column(coeffs)) / total_of(lengths)
    beyond = total_of(column(coeffs + 2) + (column(coeffs + 3) - projection) ** 2 * lengths)
    second_scale = scale_of(beyond)

    def far_second(l, c):
        near_acc[pl.ds(l, 1), :] = near_acc[pl.ds(l, 1), :] + far_row(l, parcel2)
        return c

    lax.fori_loop(0, leaves, far_second, 0)
    out_ref[1] = (near_acc[...] - projection * out_ref[0]) * second_scale

    for copies in (points_c, parcel_c, parcel2_c, tops_x, tops2_x):
        copies[2]()


def per_device(
    start, coords, area, near_list, basis, far_leaf, couple_leaf, transfer, far_top, couple_top
):
    leaves, panels = start.shape
    entries = near_list.shape[1]
    devs = lax.axis_size("dev")
    groups = lax.axis_size("group")
    smem = pl.BlockSpec(memory_space=pltpu.SMEM)
    anywhere = pl.BlockSpec(memory_space=pl.ANY)
    f32 = jnp.float32
    parcel_rows = panels // LANES * leaves + leaves + 8
    both = pl.pallas_call(
        functools.partial(kernel, devs, groups),
        out_shape=jax.ShapeDtypeStruct((2, leaves, panels), f32),
        in_specs=[smem] * 3 + [anywhere] * 7,
        out_specs=pl.BlockSpec(memory_space=pltpu.VMEM),
        scratch_shapes=[
            pltpu.VMEM(start.shape, f32),
            pltpu.VMEM(area.shape, f32),
            pltpu.VMEM(basis.shape, f32),
            pltpu.VMEM(couple_leaf.shape, f32),
            pltpu.VMEM(transfer.shape, f32),
            pltpu.VMEM(couple_top.shape, f32),
            pltpu.VMEM((devs, 3, leaves, panels), f32),
            pltpu.VMEM((devs, parcel_rows, LANES), f32),
            pltpu.VMEM((devs, parcel_rows, LANES), f32),
            pltpu.VMEM((groups * devs, 1, LANES), f32),
            pltpu.VMEM((groups * devs, 1, LANES), f32),
            pltpu.VMEM((leaves * entries, panels, panels), f32),
            pltpu.VMEM((leaves, panels), f32),
            pltpu.VMEM((leaves // 2, LANES), f32),
            pltpu.SemaphoreType.DMA((7,)),
            pltpu.SemaphoreType.DMA((3, devs)),
            pltpu.SemaphoreType.DMA((3, devs)),
            pltpu.SemaphoreType.DMA((2, groups)),
            pltpu.SemaphoreType.DMA((2, groups)),
        ],
        compiler_params=pltpu.CompilerParams(
            collective_id=0, has_side_effects=True, vmem_limit_bytes=60 * 1024 * 1024
        ),
    )(
        near_list.T, far_leaf.T, far_top, start, jnp.transpose(coords, (1, 0, 2)), area, basis,
        couple_leaf, transfer, couple_top,
    )
    return both[0], both[1]


def solution(mesh):
    rows = P(("group", "dev"), None)
    blocks = P(("group", "dev"), None, None)
    in_specs = (rows, blocks, rows, rows, blocks, rows, blocks, blocks, rows, blocks)
    return jax.shard_map(
        per_device, mesh=mesh, in_specs=in_specs, out_specs=(rows, rows), check_vma=False
    )
```

time: 54.4 us -> 41.8 us (0.77)
  local copies, waits for them, and re-layouts: 10.4 us -> 1.35 us
  Pallas kernels: 42.9 us -> 39.4 us
    unnamed x19 -> x0, local copies, waits for them, and re-layouts: 10.4 us -> none
    pallas_call x1, Pallas kernels: 42.9 us -> 39.4 us  [per_device(): pl.pallas_call(functools.partial(kernel, devs, groups), out_shape=jax.Sha...]
    squeeze x0 -> x1, local copies, waits for them, and re-layouts: none -> 1.35 us  [per_device(): return (both[0], both[1])]
where the time goes in v2:
time: 41.8 us; the launch traced here: 41.4 us
  Pallas kernels  39.4 us (94%)
  local copies, waits for them, and re-layouts  1.35 us (3%)
  between operations  0.64 us (2%)
    pallas_call x1, Pallas kernels, per_device(): pl.pallas_call(functools.partial(kernel, devs, groups), out_shape=jax.Sha...  39.4 us
    squeeze x1, local copies, waits for them, and re-layouts, per_device(): return (both[0], both[1])  1.35 us

profile of v2, /device:TPU:0, one launch (start us, length us, event | category | flops | bytes accessed | tf_op | source)
XLA Modules:
  0.0 41.4 jit_solution(2927051188075826166)
XLA Ops:
  0.6 39.4 %shard_map.113 = f32[2,16,256]{2,1,0:T(8,128)} custom-call(s32[6,16]{1,0:T(8,128)} %bitcast.8, s32[8,16]{1,0:T(8,128)} %bitcast.9, s32[1,16]{1,0:T(1,128)} %top_ref.1, f32[16,256]{1,0:T(8,128)} %start_hbm.1, f32[3,16,256]{2,1,0:T(8,128)} %bitcast.7, f32[16,256]{1,0:T(8,128)} %area_hbm.1, f32[16,64,256]{2,1,0:T(8,128)} %basis_hbm.1, ...), custom_call_target="tpu_custom_call" | custom-call | tf_op jit(solution)/shard_map/pallas_call | solution.py:361
  40.1 1.3 %slice_bitcast_fusion = (f32[16,256]{1,0:T(8,128)}, f32[16,256]{1,0:T(8,128)}) fusion(f32[2,16,256]{2,1,0:T(8,128)} %shard_map.113), kind=kLoop, calls=%fused_computation | loop fusion | bytes 65536 | tf_op jit(solution)/shard_map/squeeze | solution.py:394

commit v3 on v2

v3 whole, which is shorter than its diff:
```python
import functools
import math

import jax
import jax.numpy as jnp
from jax import lax
from jax.experimental import pallas as pl
from jax.experimental.pallas import tpu as pltpu
from jax.sharding import PartitionSpec as P

FOUR_PI = 4.0 * math.pi
SOFTENING = 0.01
EPSILON = 1e-06
LIFT = 1024.0
MESH = pl.DeviceIdType.MESH
LANES = 128


def thirds(x):
    high = x.astype(jnp.bfloat16).astype(jnp.float32)
    rest = x - high
    middle = rest.astype(jnp.bfloat16).astype(jnp.float32)
    return high, middle, rest - middle


def kernel(
    devs, groups, near_ref, far_ref, top_ref, start_hbm, coords_hbm, area_hbm, basis_hbm,
    couple_hbm, transfer_hbm, ctop_hbm, out_ref, start_ref, area_ref, basis_ref, couple_ref,
    transfer_ref, ctop_ref, points, parcel, parcel2, tops, tops2, kmat, near_acc, down_ref,
    moms, locs, aims, load_sem, send_sem, recv_sem, xsend_sem, xrecv_sem,
):
    leaves, panels = start_ref.shape
    entries = near_ref.shape[0]
    coeffs = basis_ref.shape[1]
    fars = far_ref.shape[0]
    pairs = leaves // 2
    halves = panels // LANES
    mom_row = halves * leaves
    me = lax.axis_index("dev")
    grp = lax.axis_index("group")

    def dev_peer(k):
        return (grp, lax.rem(me + k, devs))

    def grp_peer(k):
        return (lax.rem(grp + k, groups), me)

    barrier = pltpu.get_barrier_semaphore()

    def greet_dev(k, c):
        pl.semaphore_signal(barrier, inc=1, device_id=dev_peer(k), device_id_type=MESH)
        return c

    def greet_grp(k, c):
        pl.semaphore_signal(barrier, inc=1, device_id=grp_peer(k), device_id_type=MESH)
        return c

    lax.fori_loop(1, devs, greet_dev, 0)
    lax.fori_loop(1, groups, greet_grp, 0)

    loads = [
        pltpu.make_async_copy(source, target, load_sem.at[n])
        for n, (source, target) in enumerate((
            (start_hbm, start_ref), (area_hbm, area_ref), (basis_hbm, basis_ref),
            (transfer_hbm, transfer_ref), (coords_hbm, points.at[me]), (ctop_hbm, ctop_ref),
            (couple_hbm, couple_ref),
        ))
    ]
    for load in loads:
        load.start()

    def exchange(sems, count, mine, peer, source, block):
        send, recv = sems

        def copy(src, dst, k):
            return pltpu.make_async_remote_copy(
                src_ref=src, dst_ref=dst, send_sem=send(k), recv_sem=recv(k),
                device_id=peer(k), device_id_type=MESH,
            )

        def start(k, c):
            copy(source, block(mine), k).start()
            return c

        def arrive(k, c):
            landed = block(lax.rem(mine - k + count, count))
            copy(landed, landed, k).wait_recv()
            return c

        def sent(k, c):
            copy(source, block(mine), k).wait_send()
            return c

        return tuple(
            functools.partial(lax.fori_loop, 1, count, f, 0) for f in (start, arrive, sent)
        )

    def in_group(phase, source, block):
        sems = (lambda k: send_sem.at[phase, k], lambda k: recv_sem.at[phase, k])
        return exchange(sems, devs, me, dev_peer, source, block)

    def across(phase, buf):
        sems = (lambda k: xsend_sem.at[phase, k], lambda k: xrecv_sem.at[phase, k])
        return exchange(
            sems, groups, grp, grp_peer, buf.at[me * groups + grp],
            lambda g: buf.at[me * groups + g],
        )

    def line(buf):
        return lambda d: buf.at[pl.ds(d * groups, groups)]

    points_c = in_group(0, coords_hbm, lambda d: points.at[d])
    parcel_c = in_group(1, parcel.at[me], lambda d: parcel.at[d])
    parcel2_c = in_group(2, parcel2.at[me], lambda d: parcel2.at[d])
    tops_c = in_group(3, line(tops)(me), line(tops))
    tops2_c = in_group(4, line(tops2)(me), line(tops2))
    tops_x = across(0, tops)
    tops2_x = across(1, tops2)

    lane = lax.broadcasted_iota(jnp.int32, (1, LANES), 1)
    low_half = lane < coeffs
    row_r = lax.broadcasted_iota(jnp.int32, (coeffs, LANES), 0)
    lane_r = lax.broadcasted_iota(jnp.int32, (coeffs, LANES), 1)
    twice_eye = lax.rem(lane_r, coeffs) == row_r
    row_p = lax.broadcasted_iota(jnp.int32, (LANES, LANES), 0)
    lane_p = lax.broadcasted_iota(jnp.int32, (LANES, LANES), 1)
    eye = row_p == lane_p
    row8 = lax.broadcasted_iota(jnp.int32, (8, panels), 0)

    def lane_sum(x):
        total = x[:, :LANES]
        for j in range(1, x.shape[1] // LANES):
            total = total + x[:, j * LANES:(j + 1) * LANES]
        return jnp.sum(total, axis=1, keepdims=True)

    def total_of(x):
        return jnp.sum(jnp.sum(x, axis=0, keepdims=True), axis=1, keepdims=True)

    def twice_row(column):
        return jnp.sum(jnp.where(twice_eye, column, 0.0), axis=0, keepdims=True)

    def moment_row(index):
        return moms[index // leaves, pl.ds(lax.rem(index, leaves), 1), :]

    def pack(table, clusters, charges, sums):
        for h in range(halves):
            table[me, h * leaves:(h + 1) * leaves, :] = charges[:, h * LANES:(h + 1) * LANES]

        def body(i, c):
            rows = []
            for q in range(4):
                l = 4 * i + q
                total = jnp.zeros((coeffs, LANES), jnp.float32)
                for h in range(halves):
                    row = table[me, pl.ds(h * leaves + l, 1), :]
                    total = total + basis_ref[l, :, h * LANES:(h + 1) * LANES] * row
                rows.append(twice_row(lane_sum(total)))
            for q in range(4):
                moms[me, pl.ds(4 * i + q, 1), :] = rows[q]
            return c

        lax.fori_loop(0, leaves // 4, body, 0)
        table[me, mom_row:mom_row + pairs, :] = jnp.where(
            low_half, moms[me, :pairs, :], moms[me, pairs:, :]
        )
        total = jnp.zeros((coeffs, LANES), jnp.float32)
        for j in range(pairs):
            pair = jnp.where(
                low_half, moms[me, 2 * j:2 * j + 1, :], moms[me, 2 * j + 1:2 * j + 2, :]
            )
            total = total + transfer_ref[0, :, j * LANES:(j + 1) * LANES] * pair
        clusters[me * groups + grp] = jnp.where(low_half, twice_row(lane_sum(total)), sums)

    def unpack(table):
        def body(d, c):
            both = table[d, mom_row:mom_row + pairs, :]
            turned = pltpu.roll(both, coeffs, 1)
            moms[d, :pairs, :] = jnp.where(low_half, both, turned)
            moms[d, pairs:, :] = jnp.where(low_half, turned, both)
            return c

        lax.fori_loop(0, devs, body, 0)

    def cluster_row(clusters, index):
        return clusters[lax.rem(index, devs) * groups + index // devs]

    def find_down(clusters):
        total = jnp.zeros((coeffs, LANES), jnp.float32)
        for j in range(top_ref.shape[1] // 2):
            pair = jnp.where(
                low_half, cluster_row(clusters, top_ref[0, 2 * j]),
                pltpu.roll(cluster_row(clusters, top_ref[0, 2 * j + 1]), coeffs, 1),
            )
            total = total + ctop_ref[0, :, j * LANES:(j + 1) * LANES] * pair
        level = lane_sum(total)
        for j in range(pairs):
            down_ref[j:j + 1, :] = jnp.sum(
                transfer_ref[0, :, j * LANES:(j + 1) * LANES] * level, axis=0, keepdims=True
            )

    def find_local(l):
        total = jnp.zeros((coeffs, LANES), jnp.float32)
        for j in range(fars // 2):
            pair = jnp.where(
                low_half, moment_row(far_ref[2 * j, l]), moment_row(far_ref[2 * j + 1, l])
            )
            total = total + couple_ref[l, :, j * LANES:(j + 1) * LANES] * pair
        locs[l] = total

    def add_far(i, c):
        rows = []
        for q in range(4):
            l = 4 * i + q
            half = (q % 2) * coeffs
            down = down_ref[pl.ds(2 * i + q // 2, 1), :]
            total = locs[l] + jnp.where(lane_r == row_r + half, down, 0.0)
            rows.append(jnp.sum(basis_ref[l] * lane_sum(total), axis=0, keepdims=True))
        for q in range(4):
            at = pl.ds(4 * i + q, 1)
            near_acc[at, :] = near_acc[at, :] + rows[q]
        return c

    def source_of(l, n):
        own = (grp * devs + me) * leaves + l
        named = near_ref[n, l]
        named = jnp.where(named == own, near_ref[entries - 1, l], named)
        live = named >= 0
        index = jnp.where(live, named - grp * (devs * leaves), me * leaves + l)
        index = jnp.clip(index, 0, devs * leaves - 1)
        return index, jnp.where(live, 1.0 / FOUR_PI, 0.0)

    def point_rows(index):
        device, leaf = index // leaves, lax.rem(index, leaves)
        return [points[device, c, pl.ds(leaf, 1), :] for c in range(3)]

    def charge_rows(table, index, scale):
        device, leaf = index // leaves, lax.rem(index, leaves)
        return [
            table[device, pl.ds(h * leaves + leaf, 1), :] * scale for h in range(halves)
        ]

    def stack8(rows):
        total = jnp.zeros((8, panels), jnp.float32)
        for c, row in enumerate(rows):
            total = jnp.where(row8 == c, row, total)
        return total

    def to_row(acc):
        column = jnp.sum(acc, axis=1, keepdims=True)
        parts = [
            jnp.sum(
                jnp.where(eye, column[h * LANES:(h + 1) * LANES], 0.0), axis=0, keepdims=True
            )
            for h in range(panels // LANES)
        ]
        return jnp.concatenate(parts, axis=1)

    def sources_of(rows):
        x, y, z = rows
        high, middle, low = thirds(stack8((x, y, z, jnp.ones_like(x), x * x + y * y + z * z)))
        stacked = jnp.concatenate((high, middle, high, middle, low, high), axis=0)
        return stacked.astype(jnp.bfloat16)

    def coupling_of(targets, sources):
        return lax.rsqrt(jnp.dot(targets, sources, preferred_element_type=jnp.float32))

    loads[0].wait()
    loads[1].wait()
    squares = total_of(start_ref[...] * start_ref[...])
    pl.semaphore_wait(barrier, devs + groups - 2)
    points_c[0]()
    loads[2].wait()
    loads[3].wait()
    pack(parcel, tops, area_ref[...] * (start_ref[...] * LIFT), squares)
    parcel_c[0]()
    tops_x[0]()
    loads[4].wait()

    def near_self(l, c):
        rows = [points[me, axis, pl.ds(l, 1), :] for axis in range(3)]
        x, y, z = rows
        size = x * x + y * y + z * z + SOFTENING
        high, middle, low = thirds(
            stack8((-2.0 * x, -2.0 * y, -2.0 * z, size, jnp.ones_like(x)))
        )
        targets = jnp.concatenate((high, high, middle, middle, high, low), axis=0)
        targets = jnp.transpose(targets).astype(jnp.bfloat16)
        aims[l] = targets
        kmat[l * entries + entries - 1] = coupling_of(targets, sources_of(rows))
        return c

    lax.fori_loop(0, leaves, near_self, 0)
    tops_x[1]()
    tops_c[0]()
    loads[5].wait()
    loads[6].wait()
    points_c[1]()
    parcel_c[1]()
    unpack(parcel)

    def own_rows(table, l):
        return [
            table[me, pl.ds(h * leaves + l, 1), :] * (1.0 / FOUR_PI) for h in range(halves)
        ]

    def spread(acc, coupling, rows):
        for h, row in enumerate(rows):
            acc = acc + coupling[:, h * LANES:(h + 1) * LANES] * row
        return acc

    def near_first(l, c):
        acc = jnp.zeros((panels, LANES), jnp.float32)
        for n in range(entries - 1):
            index, scale = source_of(l, n)
            coupling = coupling_of(aims[l], sources_of(point_rows(index)))
            kmat[l * entries + n] = coupling
            acc = spread(acc, coupling, charge_rows(parcel, index, scale))
        acc = spread(acc, kmat[l * entries + entries - 1], own_rows(parcel, l))
        near_acc[pl.ds(l, 1), :] = to_row(acc)
        find_local(l)
        return c

    lax.fori_loop(0, leaves, near_first, 0)
    tops_c[1]()
    find_down(tops)

    panels_all = float(leaves * panels * devs * groups)

    def scale_of(total):
        return 1.0 / jnp.sqrt(total / panels_all + EPSILON)

    def pick(row, at):
        return jnp.sum(jnp.where(lane == at, row, 0.0), axis=1, keepdims=True)

    first_scale = scale_of(pick(jnp.sum(tops[...], axis=0), coeffs))

    lax.fori_loop(0, leaves // 4, add_far, 0)
    product = near_acc[...] * (first_scale * (1.0 / LIFT))
    unit = start_ref[...] * first_scale
    out_ref[0] = product
    along = total_of(unit * product)
    length = total_of(unit * unit)
    part = jnp.where(length > 0.0, along / length, 0.0)
    beyond = total_of((product - part * unit) ** 2)
    sums = jnp.where(
        lane == coeffs, along, jnp.where(lane == coeffs + 1, length, jnp.where(
            lane == coeffs + 2, beyond, part
        ))
    )
    pack(parcel2, tops2, area_ref[...] * product, sums)
    tops2_x[0]()
    parcel2_c[0]()
    tops2_x[1]()
    tops2_c[0]()
    parcel2_c[1]()
    unpack(parcel2)

    def near_second(l, c):
        acc = jnp.zeros((panels, LANES), jnp.float32)
        for n in range(entries - 1):
            index, scale = source_of(l, n)
            acc = spread(acc, kmat[l * entries + n], charge_rows(parcel2, index, scale))
        acc = spread(acc, kmat[l * entries + entries - 1], own_rows(parcel2, l))
        near_acc[pl.ds(l, 1), :] = to_row(acc)
        find_local(l)
        return c

    lax.fori_loop(0, leaves, near_second, 0)
    tops2_c[1]()
    find_down(tops2)
    rows = tops2[...].reshape(groups * devs, LANES)

    def column(at):
        return jnp.sum(jnp.where(lane == at, rows, 0.0), axis=1, keepdims=True)

    lengths = column(coeffs + 1)
    projection = total_of(column(coeffs)) / total_of(lengths)
    beyond = total_of(column(coeffs + 2) + (column(coeffs + 3) - projection) ** 2 * lengths)
    second_scale = scale_of(beyond)

    lax.fori_loop(0, leaves // 4, add_far, 0)
    out_ref[1] = (near_acc[...] - projection * out_ref[0]) * second_scale

    for copies in (
        points_c, parcel_c, parcel2_c, tops_c, tops2_c, tops_x, tops2_x
    ):
        copies[2]()


def per_device(
    start, coords, area, near_list, basis, far_leaf, couple_leaf, transfer, far_top, couple_top
):
    leaves, panels = start.shape
    entries = near_list.shape[1]
    coeffs = basis.shape[1]
    devs = lax.axis_size("dev")
    groups = lax.axis_size("group")
    smem = pl.BlockSpec(memory_space=pltpu.SMEM)
    anywhere = pl.BlockSpec(memory_space=pl.ANY)
    f32 = jnp.float32
    parcel_rows = panels // LANES * leaves + leaves // 2
    both = pl.pallas_call(
        functools.partial(kernel, devs, groups),
        out_shape=jax.ShapeDtypeStruct((2, leaves, panels), f32),
        in_specs=[smem] * 3 + [anywhere] * 7,
        out_specs=pl.BlockSpec(memory_space=pltpu.VMEM),
        scratch_shapes=[
            pltpu.VMEM(start.shape, f32),
            pltpu.VMEM(area.shape, f32),
            pltpu.VMEM(basis.shape, f32),
            pltpu.VMEM(couple_leaf.shape, f32),
            pltpu.VMEM(transfer.shape, f32),
            pltpu.VMEM(couple_top.shape, f32),
            pltpu.VMEM((devs, 3, leaves, panels), f32),
            pltpu.VMEM((devs, parcel_rows, LANES), f32),
            pltpu.VMEM((devs, parcel_rows, LANES), f32),
            pltpu.VMEM((groups * devs, 1, LANES), f32),
            pltpu.VMEM((groups * devs, 1, LANES), f32),
            pltpu.VMEM((leaves * entries, panels, panels), f32),
            pltpu.VMEM((leaves, panels), f32),
            pltpu.VMEM((leaves // 2, LANES), f32),
            pltpu.VMEM((devs, leaves, LANES), f32),
            pltpu.VMEM((leaves, coeffs, LANES), f32),
            pltpu.VMEM((leaves, panels, 48), jnp.bfloat16),
            pltpu.SemaphoreType.DMA((7,)),
            pltpu.SemaphoreType.DMA((5, devs)),
            pltpu.SemaphoreType.DMA((5, devs)),
            pltpu.SemaphoreType.DMA((2, groups)),
            pltpu.SemaphoreType.DMA((2, groups)),
        ],
        compiler_params=pltpu.CompilerParams(
            collective_id=0, has_side_effects=True, vmem_limit_bytes=60 * 1024 * 1024
        ),
    )(
        near_list.T, far_leaf.T, far_top, start, jnp.transpose(coords, (1, 0, 2)), area, basis,
        couple_leaf, transfer, couple_top,
    )
    return both[0], both[1]


def solution(mesh):
    rows = P(("group", "dev"), None)
    blocks = P(("group", "dev"), None, None)
    in_specs = (rows, blocks, rows, rows, blocks, rows, blocks, blocks, rows, blocks)
    return jax.shard_map(
        per_device, mesh=mesh, in_specs=in_specs, out_specs=(rows, rows), check_vma=False
    )
```

time: 41.8 us -> 36.4 us (0.87)
  Pallas kernels: 39.4 us -> 34.1 us
    pallas_call x1, Pallas kernels: 39.4 us -> 34.1 us  [per_device(): pl.pallas_call(functools.partial(kernel, devs, groups), out_shape=jax.Sha...]
where the time goes in v3:
time: 36.4 us; the launch traced here: 36.1 us
  Pallas kernels  34.1 us (94%)
  local copies, waits for them, and re-layouts  1.35 us (4%)
  between operations  0.64 us (2%)
    pallas_call x1, Pallas kernels, per_device(): pl.pallas_call(functools.partial(kernel, devs, groups), out_shape=jax.Sha...  34.1 us
    squeeze x1, local copies, waits for them, and re-layouts, per_device(): return (both[0], both[1])  1.35 us

profile of v3, /device:TPU:0, one launch (start us, length us, event | category | flops | bytes accessed | tf_op | source)
XLA Modules:
  0.0 36.1 jit_solution(11314359726037708476)
XLA Ops:
  0.6 34.1 %shard_map.113 = f32[2,16,256]{2,1,0:T(8,128)} custom-call(s32[6,16]{1,0:T(8,128)} %bitcast.8, s32[8,16]{1,0:T(8,128)} %bitcast.9, s32[1,16]{1,0:T(1,128)} %top_ref.1, f32[16,256]{1,0:T(8,128)} %start_hbm.1, f32[3,16,256]{2,1,0:T(8,128)} %bitcast.7, f32[16,256]{1,0:T(8,128)} %area_hbm.1, f32[16,64,256]{2,1,0:T(8,128)} %basis_hbm.1, ...), custom_call_target="tpu_custom_call" | custom-call | tf_op jit(solution)/shard_map/pallas_call | solution.py:402
  34.8 1.3 %slice_bitcast_fusion = (f32[16,256]{1,0:T(8,128)}, f32[16,256]{1,0:T(8,128)}) fusion(f32[2,16,256]{2,1,0:T(8,128)} %shard_map.113), kind=kLoop, calls=%fused_computation | loop fusion | bytes 65536 | tf_op jit(solution)/shard_map/squeeze | solution.py:438

commit v4 on v3

--- a/solution.py
+++ b/solution.py
@@ -27,7 +27,7 @@
     devs, groups, near_ref, far_ref, top_ref, start_hbm, coords_hbm, area_hbm, basis_hbm,
     couple_hbm, transfer_hbm, ctop_hbm, out_ref, start_ref, area_ref, basis_ref, couple_ref,
     transfer_ref, ctop_ref, points, parcel, parcel2, tops, tops2, kmat, near_acc, down_ref,
-    moms, locs, aims, load_sem, send_sem, recv_sem, xsend_sem, xrecv_sem,
+    moms, locs, aims, kself, load_sem, send_sem, recv_sem, xsend_sem, xrecv_sem,
 ):
     leaves, panels = start_ref.shape
     entries = near_ref.shape[0]
@@ -286,7 +286,7 @@
         targets = jnp.concatenate((high, high, middle, middle, high, low), axis=0)
         targets = jnp.transpose(targets).astype(jnp.bfloat16)
         aims[l] = targets
-        kmat[l * entries + entries - 1] = coupling_of(targets, sources_of(rows))
+        kself[l] = coupling_of(targets, sources_of(rows))
         return c
 
     lax.fori_loop(0, leaves, near_self, 0)
@@ -308,19 +308,24 @@
             acc = acc + coupling[:, h * LANES:(h + 1) * LANES] * row
         return acc
 
-    def near_first(l, c):
-        acc = jnp.zeros((panels, LANES), jnp.float32)
-        for n in range(entries - 1):
-            index, scale = source_of(l, n)
-            coupling = coupling_of(aims[l], sources_of(point_rows(index)))
-            kmat[l * entries + n] = coupling
-            acc = spread(acc, coupling, charge_rows(parcel, index, scale))
-        acc = spread(acc, kmat[l * entries + entries - 1], own_rows(parcel, l))
-        near_acc[pl.ds(l, 1), :] = to_row(acc)
-        find_local(l)
-        return c
-
-    lax.fori_loop(0, leaves, near_first, 0)
+    def near_first(i, c):
+        rows = []
+        for q in range(4):
+            l = 4 * i + q
+            acc = jnp.zeros((panels, LANES), jnp.float32)
+            for n in range(entries - 1):
+                index, scale = source_of(l, n)
+                coupling = coupling_of(aims[l], sources_of(point_rows(index)))
+                kmat[l * (entries - 1) + n] = coupling
+                acc = spread(acc, coupling, charge_rows(parcel, index, scale))
+            acc = spread(acc, kself[l], own_rows(parcel, l))
+            rows.append(to_row(acc))
+            find_local(l)
+        for q in range(4):
+            near_acc[pl.ds(4 * i + q, 1), :] = rows[q]
+        return c
+
+    lax.fori_loop(0, leaves // 4, near_first, 0)
     tops_c[1]()
     find_down(tops)
 
@@ -355,17 +360,23 @@
     parcel2_c[1]()
     unpack(parcel2)
 
-    def near_second(l, c):
-        acc = jnp.zeros((panels, LANES), jnp.float32)
-        for n in range(entries - 1):
-            index, scale = source_of(l, n)
-            acc = spread(acc, kmat[l * entries + n], charge_rows(parcel2, index, scale))
-        acc = spread(acc, kmat[l * entries + entries - 1], own_rows(parcel2, l))
-        near_acc[pl.ds(l, 1), :] = to_row(acc)
-        find_local(l)
-        return c
-
-    lax.fori_loop(0, leaves, near_second, 0)
+    def near_second(i, c):
+        rows = []
+        for q in range(4):
+            l = 4 * i + q
+            acc = jnp.zeros((panels, LANES), jnp.float32)
+            for n in range(entries - 1):
+                index, scale = source_of(l, n)
+                at = l * (entries - 1) + n
+                acc = spread(acc, kmat[at], charge_rows(parcel2, index, scale))
+            acc = spread(acc, kself[l], own_rows(parcel2, l))
+            rows.append(to_row(acc))
+            find_local(l)
+        for q in range(4):
+            near_acc[pl.ds(4 * i + q, 1), :] = rows[q]
+        return c
+
+    lax.fori_loop(0, leaves // 4, near_second, 0)
     tops2_c[1]()
     find_down(tops2)
     rows = tops2[...].reshape(groups * devs, LANES)
@@ -416,12 +427,13 @@
             pltpu.VMEM((devs, parcel_rows, LANES), f32),
             pltpu.VMEM((groups * devs, 1, LANES), f32),
             pltpu.VMEM((groups * devs, 1, LANES), f32),
-            pltpu.VMEM((leaves * entries, panels, panels), f32),
+            pltpu.VMEM((leaves * (entries - 1), panels, panels), f32),
             pltpu.VMEM((leaves, panels), f32),
             pltpu.VMEM((leaves // 2, LANES), f32),
             pltpu.VMEM((devs, leaves, LANES), f32),
             pltpu.VMEM((leaves, coeffs, LANES), f32),
             pltpu.VMEM((leaves, panels, 48), jnp.bfloat16),
+            pltpu.VMEM((leaves, panels, panels), f32),
             pltpu.SemaphoreType.DMA((7,)),
             pltpu.SemaphoreType.DMA((5, devs)),
             pltpu.SemaphoreType.DMA((5, devs)),

time: 36.4 us -> 32.8 us (0.901)
  Pallas kernels: 34.1 us -> 30.5 us
    pallas_call x1, Pallas kernels: 34.1 us -> 30.5 us  [per_device(): pl.pallas_call(functools.partial(kernel, devs, groups), out_shape=jax.Sha...]
where the time goes in v4:
time: 32.8 us; the launch traced here: 32.5 us
  Pallas kernels  30.5 us (93%)
  local copies, waits for them, and re-layouts  1.35 us (4%)
  between operations  0.64 us (2%)
    pallas_call x1, Pallas kernels, per_device(): pl.pallas_call(functools.partial(kernel, devs, groups), out_shape=jax.Sha...  30.5 us
    squeeze x1, local copies, waits for them, and re-layouts, per_device(): return (both[0], both[1])  1.35 us

profile of v4, /device:TPU:0, one launch (start us, length us, event | category | flops | bytes accessed | tf_op | source)
XLA Modules:
  0.0 32.5 jit_solution(18086219914235847275)
XLA Ops:
  0.6 30.5 %shard_map.113 = f32[2,16,256]{2,1,0:T(8,128)} custom-call(s32[6,16]{1,0:T(8,128)} %bitcast.8, s32[8,16]{1,0:T(8,128)} %bitcast.9, s32[1,16]{1,0:T(1,128)} %top_ref.1, f32[16,256]{1,0:T(8,128)} %start_hbm.1, f32[3,16,256]{2,1,0:T(8,128)} %bitcast.7, f32[16,256]{1,0:T(8,128)} %area_hbm.1, f32[16,64,256]{2,1,0:T(8,128)} %basis_hbm.1, ...), custom_call_target="tpu_custom_call" | custom-call | tf_op jit(solution)/shard_map/pallas_call | solution.py:413
  31.2 1.3 %slice_bitcast_fusion = (f32[16,256]{1,0:T(8,128)}, f32[16,256]{1,0:T(8,128)}) fusion(f32[2,16,256]{2,1,0:T(8,128)} %shard_map.113), kind=kLoop, calls=%fused_computation | loop fusion | bytes 65536 | tf_op jit(solution)/shard_map/squeeze | solution.py:450
